TPU v7x, 256 devices: a whole 4x4x8 slice. The times are simulated.
256 devices in a mesh: hit: 64 (over x, z, y_hi), conf: 4 (over y_lo, core).
Axes of the slice: x: 4, y: 4 (y_hi: 2, y_lo: 2; y = y_hi * 2 + y_lo), z: 8, core: 2. Of those that a mesh axis runs over, the one named last changes fastest.
Arguments:
- scores: bfloat16 [393216, 1024], P('hit', 'conf'), may hold values from -44 to 44, as said below
- conf_init: bfloat16 [1024, 256], P('conf'), may hold values from -0.625 to 0.625
Outputs:
- hit_factors: float32 [393216, 256], P(('hit', 'conf'))
- conf_factors: float32 [1024, 256], P('conf')
Inputs may be any that keep to these rules, and one draw needn't show every extreme that they name: real-valued docking scores.
All inputs are finite; a program needn't handle non-finite values.
Results may differ from a plain program's by a relative error of at most 0.0015.
Values may be sent and summed in bfloat16 or wider, within the bound.
A program may use at most 64 MiB of HBM per device.

v0:
```python
import jax
import jax.numpy as jnp
from jax import lax
from jax.sharding import PartitionSpec as P


def solve_right(rhs, gram, ridge_term):
    identity = jnp.eye(gram.shape[0], dtype=jnp.float32)
    factor = jnp.linalg.cholesky(gram + ridge_term * identity)
    halfway = jax.scipy.linalg.solve_triangular(factor, rhs.T, lower=True)
    return jax.scipy.linalg.solve_triangular(factor, halfway, lower=True, trans=1).T


def gram_of(matrix):
    return lax.dot_general(
        matrix, matrix, (((0,), (0,)), ((), ())), preferred_element_type=jnp.float32
    )


def cross_of(left, right):
    return lax.dot_general(
        left, right, (((0,), (0,)), ((), ())), preferred_element_type=jnp.float32
    )


def shards(scores, conf_init):
    total_hits = scores.shape[0] * lax.axis_size("hit")
    gram_conf = lax.psum(gram_of(conf_init), "conf")
    tile_rows = scores
    rhs_hit = lax.psum_scatter(
        jnp.dot(tile_rows, conf_init, preferred_element_type=jnp.float32),
        "conf",
        scatter_dimension=0,
        tiled=True,
    )
    hit_factors = solve_right(rhs_hit, gram_conf, 0.5)
    hit_rounded = hit_factors.astype(jnp.bfloat16)
    tile_rows = scores
    rhs_part = cross_of(tile_rows, lax.all_gather(hit_rounded, "conf", axis=0, tiled=True))
    gram_hit = lax.psum(gram_of(hit_rounded), ("hit", "conf"))
    rhs_conf = lax.psum(rhs_part, "hit")
    conf_factors = solve_right(rhs_conf, gram_hit, 0.5 * total_hits)
    return (hit_factors, conf_factors)


def solution(mesh):
    placed = (P("hit", "conf"), P("conf", None))
    return jax.shard_map(
        shards,
        mesh=mesh,
        in_specs=placed,
        out_specs=(P(("hit", "conf"), None), P("conf", None)),
        check_vma=False,
    )
```

profile of v0, /device:TPU:6, one launch (start us, length us, event | category | flops | bytes accessed | tf_op | source)
XLA Modules:
  0.0 1072.2 jit_solution(17376263735409556139)
XLA Ops:
  7.2 2.0 fusion.25
  9.4 4.5 fusion.26
  14.0 41.3 %all-reduce.5.cloned.1.call-done = f32[256,256]{0,1:T(8,128)} async-done(((f32[256,256]{0,1:T(8,128)}), f32[256,256]{0,1:T(8,128)}) %all-reduce.5.cloned.1.call-update) | async-done | bytes 262160 | tf_op jit(solution)/shard_map/psum | solution.py:28
  55.3 1.7 select_add_fusion.1
  57.0 1.1 copy.5
  58.1 1.0 fusion.3
  59.1 0.7 copy-done.3
  59.8 11.7 %cholesky.130 = f32[128,128]{1,0:T(8,128)S(1)} custom-call(f32[128,128]{1,0:T(8,128)S(1)} %cholesky.194), custom_call_target="Cholesky" | custom-call | tf_op jit(solution)/shard_map/jit(cholesky)/cholesky | solution.py:9
  71.6 9.8 custom-call.25
  81.5 1.0 fusion.8
  82.6 1.1 convolution_subtract_fusion.5
  83.7 11.7 %cholesky.147 = f32[128,128]{1,0:T(8,128)S(1)} custom-call(f32[128,128]{1,0:T(8,128)S(1)} %convolution_subtract_fusion.5), custom_call_target="Cholesky" | custom-call | tf_op jit(solution)/shard_map/jit(cholesky)/cholesky | solution.py:9
  95.5 0.7 cholesky.155
  96.3 0.7 compare_reduce_fusion.2
  98.3 0.6 constant_dynamic-update-slice_fusion.3
  98.9 0.6 constant_dynamic-update-slice_fusion.2
  99.5 1.0 select_select_fusion.1
  100.6 0.7 broadcast.146.clone
  101.2 5.5 while.2
  101.3 0.6 fusion.53
  101.9 1.3 dynamic-slice.13
  103.3 0.6 bitcast_dynamic-update-slice_fusion.4
  104.0 0.6 fusion.53
  104.6 1.3 dynamic-slice.13
  106.1 0.6 bitcast_dynamic-update-slice_fusion.4
  106.7 20.5 %custom-call.22 = f32[2,128,128]{1,2,0:T(8,128)S(1)} custom-call(f32[2,128,128]{2,1,0:T(8,128)} %get-tuple-element.10), custom_call_target="InvertDiagBlocksLowerTriangular" | custom-call | tf_op jit(solution)/shard_map/jit(_solve_triangular)/triangular_solve | solution.py:11
  127.2 2.0 fusion
  129.2 2.5 convolution_subtract_fusion.1
  131.8 0.9 fusion.14
  132.6 0.8 fusion.13
  133.4 0.8 convolution_subtract_fusion
  134.2 0.8 fusion.12
  135.0 0.9 copy-done.2
  136.0 1.0 fusion.22
  136.9 2.5 fusion.27
  140.3 2.6 maximum_bitcast_fusion
  142.9 3.0 copy.16
  146.0 245.0 %all-reduce.7.cloned.1.call-done = f32[256,256]{0,1:T(8,128)} async-done(((f32[256,256]{0,1:T(8,128)}), f32[256,256]{0,1:T(8,128)}) %all-reduce.7.cloned.1.call-update) | async-done | bytes 262160 | tf_op jit(solution)/shard_map/psum | solution.py:40
  390.9 1.7 select_add_fusion
  392.6 1.1 copy.11
  393.7 1.0 fusion.2
  394.7 0.7 copy-done.4
  395.4 11.7 %cholesky.164 = f32[128,128]{1,0:T(8,128)S(1)} custom-call(f32[128,128]{1,0:T(8,128)S(1)} %cholesky.197), custom_call_target="Cholesky" | custom-call | tf_op jit(solution)/shard_map/jit(cholesky)/cholesky | solution.py:9
  407.2 9.8 custom-call.26
  417.1 1.0 fusion.6
  418.2 1.1 convolution_subtract_fusion.4
  419.3 11.7 %cholesky.181 = f32[128,128]{1,0:T(8,128)S(1)} custom-call(f32[128,128]{1,0:T(8,128)S(1)} %convolution_subtract_fusion.4), custom_call_target="Cholesky" | custom-call | tf_op jit(solution)/shard_map/jit(cholesky)/cholesky | solution.py:9
  431.1 0.7 cholesky.189
  432.5 0.6 compare_reduce_fusion
  434.3 0.6 constant_dynamic-update-slice_fusion.1
  435.6 1.0 select_select_fusion
  436.6 3.6 fusion.28
  440.2 0.7 broadcast.146
  440.9 5.5 while.3
  440.9 0.6 fusion.54
  441.5 1.3 dynamic-slice.15
  443.6 0.6 fusion.54
  444.2 1.3 dynamic-slice.15
  445.7 0.6 bitcast_dynamic-update-slice_fusion.5
  446.3 20.5 %custom-call.23 = f32[2,128,128]{1,2,0:T(8,128)S(1)} custom-call(f32[2,128,128]{2,1,0:T(8,128)} %get-tuple-element.18), custom_call_target="InvertDiagBlocksLowerTriangular" | custom-call | tf_op jit(solution)/shard_map/jit(_solve_triangular)/triangular_solve | solution.py:11
  466.8 594.5 %all-reduce.9.cloned.1.call-done = f32[256,256]{1,0:T(8,128)} async-done(((f32[256,256]{1,0:T(8,128)}), f32[256,256]{1,0:T(8,128)}) %all-reduce.9.cloned.1.call-update) | async-done | bytes 262160 | tf_op jit(solution)/shard_map/psum | solution.py:41
  1061.3 1.2 fusion.4
  1062.5 1.2 convolution_subtract_fusion.3
  1064.8 0.8 copy.17
  (49 shorter events, 5.2 us)
Async XLA Ops:
  7.2 2.2 copy-start
  7.2 48.2 %all-reduce.5.cloned.1.call-start = ((), (), s32[]{:S(2)}) async-start(), calls=%async_computation.1 | async-start | bytes 524288 | tf_op jit(solution)/shard_map/psum | solution.py:28
  9.3 117.9 %reduce-scatter.2.cloned.1.call-start = ((), (), s32[]{:S(2)}) async-start(), calls=%async_computation.2 | async-start | bytes 7864320 | tf_op jit(solution)/shard_map/reduce_scatter | solution.py:30
  13.9 377.0 %all-reduce.7.cloned.1.call-start = ((), (), s32[]{:S(2)}) async-start(), calls=%async_computation.3 | async-start | bytes 524288 | tf_op jit(solution)/shard_map/psum | solution.py:40
  59.1 0.7 copy-start.3
  133.4 1.6 copy-start.1
  135.0 0.9 copy-start.2
  139.5 297.1 %all-gather.2.cloned.1.call-start = ((), (), s32[]{:S(2)}) async-start(), calls=%async_computation.4 | async-start | bytes 3932160 | tf_op jit(solution)/shard_map/all_gather | solution.py:39
  140.1 921.2 %all-reduce.9.cloned.1.call-start = ((), (), s32[]{:S(2)}) async-start(), calls=%async_computation.5 | async-start | bytes 524288 | tf_op jit(solution)/shard_map/psum | solution.py:41
  394.7 0.7 copy-start.4
Sparse Core Ops, SparseCore 0:
  11.2 44.0 all-reduce.4
  58.1 66.0 reduce-scatter.1
  139.6 251.2 all-reduce.6
  392.7 38.7 all-gather.1
  440.3 620.9 all-reduce.8
where the time goes:
time: 1090 us; the launch traced here: 1070 us
  waiting for transfers between devices  881 us (81%)
  other arithmetic  120 us (11%)
  matrix products  28.2 us (3%)
  local copies, waits for them, and re-layouts  25.2 us (2%)
  between operations  16.5 us (2%)
    psum x1, waiting for transfers between devices, shards(): rhs_conf = lax.psum(rhs_part, 'hit')  594 us
    psum x1, waiting for transfers between devices, shards(): gram_hit = lax.psum(gram_of(hit_rounded), ('hit', 'conf'))  245 us
    another operation x13, other arithmetic, solve_right(): factor = jnp.linalg.cholesky(gram + ridge_term * identity)  68.6 us
    another operation x5, other arithmetic, solve_right(): jax.scipy.linalg.solve_triangular(factor, halfway, lower=True, trans=1)  42.9 us
    psum x1, waiting for transfers between devices, shards(): gram_conf = lax.psum(gram_of(conf_init), 'conf')  41.3 us
  transfers between devices with their start and end apart: 5, of which 3 were waited for; matrix products, arithmetic and copies ran while one was open for 14% of the time, Pallas kernels for 0%

commit v1 on v0

v1 whole, which is shorter than its diff:
```python
import jax
import jax.numpy as jnp
from jax import lax
from jax.experimental import pallas as pl
from jax.experimental.pallas import tpu as pltpu
from jax.sharding import PartitionSpec as P

MESH = pl.DeviceIdType.MESH
F32 = jnp.float32
BF16 = jnp.bfloat16
NX, NZ = 4, 8
CH = 256


def exact_dot(a, b):
    return jnp.dot(a, b, precision=lax.Precision.HIGHEST, preferred_element_type=F32)


def scaled_steps(low, count):
    scales = []
    for _ in range(count):
        scales.append(2.0 / (1.0 + low))
        low = 4.0 * low / (1.0 + low) ** 2
    return scales


class Inverse:
    def __init__(self, a, low, scaled, corrected):
        n = a.shape[0]
        rows = lax.broadcasted_iota(jnp.int32, (n, n), 0)
        cols = lax.broadcasted_iota(jnp.int32, (n, n), 1)
        self.eye = (rows == cols).astype(F32)
        self.unscale = 1.0 / jnp.sqrt(jnp.sum(a * a, axis=(0, 1), keepdims=True))
        self.a = a * self.unscale
        self.scales = scaled_steps(low, scaled)
        self.corrected = corrected
        s = self.scales[0]
        self.x = (2.0 * s) * self.eye - (s * s) * self.a
        self.y = (2.0 * s) * self.a - (s * s) * exact_dot(self.a, self.a)

    def run(self, first, last):
        for s in self.scales[first:last]:
            m = (2.0 * s) * self.eye - (s * s) * self.y
            self.x, self.y = exact_dot(self.x, m), exact_dot(self.y, m)

    def finish(self):
        x = self.x
        for _ in range(self.corrected):
            x = exact_dot(x, 2.0 * self.eye - exact_dot(self.a, x))
        return x * self.unscale


def kernel(
    ridge_conf,
    ridge_hit,
    scores,
    conf_init,
    hit_out,
    conf_out,
    s_buf,
    c_buf,
    z_buf,
    g_acc,
    t_acc,
    g_core,
    g_half,
    g_xy,
    g_z,
    g_full,
    t_core,
    t_y,
    r_x,
    r_part,
    r_zy,
    r_full,
    cs, cr, ss, sr, sl, os,
    g1s, g1r, g2s, g2r, g3s, g3r, g4s, g4r, g5s, g5r,
    h1s, h1r, h2s, h2r, h3s, h3r, h4s, h4r, h5s, h5r, h6s, h6r,
):
    own = s_buf.shape[1]
    chunks = own // CH
    hit = lax.axis_index("hit")
    conf = lax.axis_index("conf")
    x = hit // (2 * NZ)
    z = (hit // 2) % NZ
    yh = hit % 2
    yl = conf // 2
    core = conf % 2

    def device(x_, yh_, z_, yl_, core_):
        return ((x_ * NZ + z_) * 2 + yh_, yl_ * 2 + core_)

    plane = x * 4 + yh * 2 + yl
    column = z * 2 + yh

    def plane_peer(r):
        p = (plane + r) % 16
        return p, device(p // 4, (p // 2) % 2, z, p % 2, core)

    def z_peer(r):
        return device(x, yh, (z + r) % NZ, yl, core)

    def column_peer(r):
        p = (column + r) % 16
        return p, device(x, p % 2, p // 2, yl, core)

    def x_peer(r):
        p = (x + r) % NX
        return p, device(p, yh, z, yl, core)

    group_conf = [conf, yl * 2 + 1 - core, (1 - yl) * 2 + core, (1 - yl) * 2 + 1 - core]
    group = [(hit, c) for c in group_conf]

    barrier = pltpu.get_barrier_semaphore()

    def greet(to):
        pl.semaphore_signal(barrier, inc=1, device_id=to, device_id_type=MESH)

    greet(group[1])
    greet(group[3])

    @pl.loop(1, 16)
    def _(r):
        greet(plane_peer(r)[1])

    @pl.loop(1, NZ)
    def _(r):
        greet(z_peer(r))
        greet(device(x, 1 - yh, (z + r) % NZ, yl, core))

    pl.semaphore_wait(barrier, 2 + 15 + 2 * (NZ - 1))

    def send(src, dst, send_sem, recv_sem, to):
        copy = pltpu.make_async_remote_copy(
            src_ref=src, dst_ref=dst, send_sem=send_sem, recv_sem=recv_sem, device_id=to, device_id_type=MESH
        )
        return copy

    def rows(start, size):
        return pl.ds(pl.multiple_of(start, size), size)

    conf_copies = [send(conf_init, c_buf.at[d], cs.at[d], cr.at[d], group[d]) for d in (1, 2)]
    for copy in conf_copies:
        copy.start()

    def score_copy(d, i):
        return send(
            scores.at[rows(group_conf[d] * own + i * CH, CH)],
            s_buf.at[d, rows(i * CH, CH)],
            ss.at[d, i],
            sr.at[d, i],
            group[d],
        )

    mine = pltpu.make_async_copy(scores.at[rows(conf * own, own)], s_buf.at[0], sl.at[0])
    mine.start()

    @pl.loop(0, chunks)
    def _(i):
        for d in (2, 3, 1):
            score_copy(d, i).start()

    conf_copies[1].wait()
    passed_on = send(c_buf.at[2], c_buf.at[3], cs.at[3], cr.at[3], group[1])
    passed_on.start()
    conf_copies[0].wait()
    passed_on.wait()
    c_buf[0] = conf_init[...]

    def square(m):
        return lax.dot_general(m, m, (((0,), (0,)), ((), ())), preferred_element_type=F32)

    def ridged(gram, ridge):
        n = gram.shape[0]
        r_ = lax.broadcasted_iota(jnp.int32, (n, n), 0)
        c_ = lax.broadcasted_iota(jnp.int32, (n, n), 1)
        return gram + jnp.where(r_ == c_, F32(ridge), F32(0.0))

    gram_conf = (square(c_buf[0]) + square(c_buf[1])) + (square(c_buf[2]) + square(c_buf[3]))
    inverse = Inverse(ridged(gram_conf, ridge_conf), 4.8e-6, 11, 2)
    inverse.run(1, 11)
    g_full[...] = inverse.finish()

    g_acc[...] = jnp.zeros_like(g_acc)
    t_acc[...] = jnp.zeros_like(t_acc)
    mine.wait()

    def out_copy(i):
        part = rows(i * CH, CH)
        return pltpu.make_async_copy(z_buf.at[part], hit_out.at[part], os.at[i])

    @pl.loop(0, chunks)
    def _(i):
        part = rows(i * CH, CH)
        for d in (1, 2, 3):
            score_copy(d, i).wait()
        rhs = jnp.zeros((CH, 256), F32)
        for d in range(4):
            rhs += jnp.dot(s_buf[d, part, :], c_buf[d], preferred_element_type=F32)
        solved = exact_dot(rhs, g_full[...])
        z_buf[part, :] = solved
        out_copy(i).start()
        rounded = solved.astype(BF16)
        turned = solved.T.astype(BF16)
        g_acc[...] += jnp.dot(turned, rounded, preferred_element_type=F32)
        for d in range(4):
            t_acc[d] += jnp.dot(turned, s_buf[d, part, :], preferred_element_type=F32)

    half = rows(core * 128, 128)
    other_half = rows((1 - core) * 128, 128)
    g1 = send(g_acc.at[other_half], g_core, g1s.at[0], g1r.at[0], group[1])
    g1.start()
    h1 = [send(t_acc.at[2 * k + 1], t_core.at[k], h1s.at[k], h1r.at[k], group[1]) for k in (1, 0)]
    for copy in h1:
        copy.start()

    g1.wait()
    g_half[...] = g_acc[half, :] + g_core[...]

    def g2(r):
        p, to = plane_peer(r)
        return send(g_half.at[rows(p * 8, 8)], g_xy.at[r], g2s.at[r], g2r.at[r], to)

    @pl.loop(1, 16)
    def _(r):
        g2(r).start()

    h1[0].wait()
    t_acc[2] += t_core[1]
    h2 = send(t_acc.at[2], t_y, h2s.at[0], h2r.at[0], group[2])
    h2.start()
    h1[1].wait()
    t_acc[0] += t_core[0]

    g_xy[0] = g_half[rows(plane * 8, 8), :]

    @pl.loop(1, 16)
    def _(r):
        g2(r).wait()

    g_z[z] = jnp.sum(g_xy[...], axis=0)

    def g3(r):
        return send(g_z.at[z], g_z.at[z], g3s.at[r], g3r.at[r], z_peer(r))

    @pl.loop(1, NZ)
    def _(r):
        g3(r).start()

    @pl.loop(1, NZ)
    def _(r):
        g3(r).wait()

    kept = rows(core * 128 + plane * 8, 8)
    g_full[kept, :] = jnp.sum(g_z[...], axis=0)

    def g4(r):
        return send(g_full.at[kept], g_full.at[kept], g4s.at[r], g4r.at[r], plane_peer(r)[1])

    @pl.loop(1, 16)
    def _(r):
        g4(r).start()

    @pl.loop(1, 16)
    def _(r):
        g4(r).wait()

    g5 = send(g_full.at[half], g_full.at[half], g5s.at[0], g5r.at[0], group[1])
    g5.start()

    h2.wait()
    t_acc[0] += t_y[...]

    def h3(r):
        p, to = x_peer(r)
        return send(t_acc.at[0, rows(p * 64, 64)], r_x.at[r], h3s.at[r], h3r.at[r], to)

    for r in (1, 3, 2):
        h3(r).start()

    g5.wait()
    inverse = Inverse(ridged(g_full[...], ridge_hit), 4.9e-7, 12, 2)
    inverse.run(1, 3)

    for r in (1, 3, 2):
        h3(r).wait()
    r_part[...] = (t_acc[0, rows(x * 64, 64), :] + r_x[1]) + (r_x[2] + r_x[3])

    def h4(r):
        p, to = column_peer(r)
        return send(
            r_part.at[rows(p // 2 * 8, 8), rows(p % 2 * 128, 128)], r_zy.at[r], h4s.at[r], h4r.at[r], to
        )

    @pl.loop(1, 16)
    def _(r):
        h4(r).start()

    inverse.run(3, 6)

    r_zy[0] = r_part[rows(z * 8, 8), rows(yh * 128, 128)]

    @pl.loop(1, 16)
    def _(r):
        h4(r).wait()

    piece = (rows(x * 64 + z * 8, 8), rows(yh * 128, 128))
    r_full[piece] = jnp.sum(r_zy[...], axis=0)

    def h5(r):
        return send(r_full.at[piece], r_full.at[piece], h5s.at[r], h5r.at[r], column_peer(r)[1])

    @pl.loop(1, 16)
    def _(r):
        h5(r).start()

    inverse.run(6, 9)

    @pl.loop(1, 16)
    def _(r):
        h5(r).wait()

    def h6(r):
        block = rows(x * 64, 64)
        return send(r_full.at[block], r_full.at[block], h6s.at[r], h6r.at[r], x_peer(r)[1])

    for r in (1, 3, 2):
        h6(r).start()

    inverse.run(9, 12)
    solver = inverse.finish()

    for r in (1, 3, 2):
        h6(r).wait()
    conf_out[...] = exact_dot(r_full[...].T, solver)

    @pl.loop(0, chunks)
    def _(i):
        out_copy(i).wait()


def shards(scores, conf_init):
    hits, confs = scores.shape
    rank = conf_init.shape[1]
    own = hits // 4
    chunks = own // CH
    total_hits = hits * lax.axis_size("hit")
    vmem = pltpu.VMEM
    dma = pltpu.SemaphoreType.DMA

    def body(*refs):
        kernel(0.5, 0.5 * total_hits, *refs)

    return pl.pallas_call(
        body,
        out_shape=(
            jax.ShapeDtypeStruct((own, rank), F32),
            jax.ShapeDtypeStruct((confs, rank), F32),
        ),
        in_specs=[pl.BlockSpec(memory_space=pl.ANY), pl.BlockSpec(memory_space=pltpu.VMEM)],
        out_specs=(pl.BlockSpec(memory_space=pl.ANY), pl.BlockSpec(memory_space=pltpu.VMEM)),
        scratch_shapes=[
            vmem((4, own, confs), BF16),
            vmem((4, confs, rank), BF16),
            vmem((own, rank), F32),
            vmem((rank, rank), F32),
            vmem((4, rank, confs), F32),
            vmem((128, rank), F32),
            vmem((128, rank), F32),
            vmem((16, 8, rank), F32),
            vmem((NZ, 8, rank), F32),
            vmem((rank, rank), F32),
            vmem((2, rank, confs), F32),
            vmem((rank, confs), F32),
            vmem((NX, 64, confs), F32),
            vmem((64, confs), F32),
            vmem((16, 8, 128), F32),
            vmem((rank, confs), F32),
            dma((4,)), dma((4,)), dma((4, chunks)), dma((4, chunks)), dma((1,)), dma((chunks,)),
            dma((1,)), dma((1,)), dma((16,)), dma((16,)), dma((NZ,)), dma((NZ,)), dma((16,)), dma((16,)), dma((1,)), dma((1,)),
            dma((2,)), dma((2,)), dma((1,)), dma((1,)), dma((NX,)), dma((NX,)), dma((16,)), dma((16,)), dma((16,)), dma((16,)),
            dma((NX,)), dma((NX,)),
        ],
        compiler_params=pltpu.CompilerParams(
            collective_id=0, has_side_effects=True, vmem_limit_bytes=40 * 1024 * 1024
        ),
    )(scores, conf_init)


def solution(mesh):
    return jax.shard_map(
        shards,
        mesh=mesh,
        in_specs=(P("hit", "conf"), P("conf", None)),
        out_specs=(P(("hit", "conf"), None), P("conf", None)),
        check_vma=False,
    )
```

time: 1090 us -> 98.4 us (0.09); the launches traced: 1070 us -> 98 us
  waiting for transfers between devices: 881 us -> 0 us
  other arithmetic: 120 us -> 0 us
  Pallas kernels: 0 us -> 92.7 us
  matrix products: 28.2 us -> 0 us
  local copies, waits for them, and re-layouts: 25.2 us -> 4.63 us
  between operations: 16.5 us -> 0.65 us
    psum x3 -> x0, waiting for transfers between devices: 881 us -> none  [the longest x1 594 us: shards(): rhs_conf = lax.psum(rhs_part, 'hit')]
    another operation x18 -> x0, other arithmetic: 111 us -> none  [the longest x13 68.6 us: solve_right(): factor = jnp.linalg.cholesky(gram + ridge_term * identity)]
    pallas_call x0 -> x1, Pallas kernels: none -> 92.7 us  [shards(): pl.pallas_call(body, out_shape=(jax.ShapeDtypeStruct((own, rank), F32), j...]
    another operation x16 -> x0, matrix products: 15.5 us -> none  [the longest x6 8.12 us: solve_right(): halfway = jax.scipy.linalg.solve_triangular(factor, rhs.T, lower=True)]
    another operation x35 -> x0, local copies, waits for them, and re-layouts: 15.5 us -> none
    dot_general x4 -> x0, matrix products: 12.7 us -> none  [the longest x2 4.56 us: gram_of(): lax.dot_general(matrix, matrix, (((0,), (0,)), ((), ())), preferred_eleme...]
  transfers between devices with their start and end apart: 5 -> 0, of which waited for: 3 -> 0; matrix products, arithmetic and copies ran while one was open for 14% -> 0% of each run, Pallas kernels for 0% -> 0%
where the time goes in v1:
time: 98.4 us; the launch traced here: 98 us
  Pallas kernels  92.7 us (94%)
  local copies, waits for them, and re-layouts  4.63 us (5%)
    pallas_call x1, Pallas kernels, shards(): pl.pallas_call(body, out_shape=(jax.ShapeDtypeStruct((own, rank), F32), j...  92.7 us
    unnamed x6, local copies, waits for them, and re-layouts  4.63 us

profile of v1, /device:TPU:6, one launch (start us, length us, event | category | flops | bytes accessed | tf_op | source)
XLA Modules:
  0.0 98.0 jit_solution(8847191580990238218)
XLA Ops:
  0.6 0.0 copy-start
  0.6 1.9 %copy-done = bf16[6144,256]{1,0:T(8,128)(2,1)S(1)} copy-done((bf16[6144,256]{1,0:T(8,128)(2,1)S(1)}, bf16[6144,256]{1,0:T(8,128)(2,1)}, u32[]{:S(2)}) %copy-start) | copy-done | bytes 3145752
  2.5 0.0 copy-start.1
  2.5 0.9 copy-done.1
  3.4 92.7 %shard_map.41 = (f32[1536,256]{1,0:T(8,128)S(1)}, f32[256,256]{1,0:T(8,128)S(1)}) custom-call(bf16[6144,256]{1,0:T(8,128)(2,1)S(1)} %copy-done, bf16[256,256]{1,0:T(8,128)(2,1)S(1)} %copy-done.1), custom_call_target="tpu_custom_call" | custom-call | tf_op jit(solution)/shard_map/pallas_call | solution.py:354
  96.1 1.1 %copy.6 = f32[1536,256]{1,0:T(8,128)} copy(f32[1536,256]{1,0:T(8,128)S(1)} %get-tuple-element.4) | data formatting | bytes 3145728
  97.3 0.7 copy.7
Async XLA Ops:
  0.6 1.9 %copy-start = (bf16[6144,256]{1,0:T(8,128)(2,1)S(1)}, bf16[6144,256]{1,0:T(8,128)(2,1)}, u32[]{:S(2)}) copy-start(bf16[6144,256]{1,0:T(8,128)(2,1)} %refs_0_.1) | copy-start | bytes 9437188
  2.5 0.9 copy-start.1

commit v2 on v1

v2 whole, which is shorter than its diff:
```python
import jax
import jax.numpy as jnp
from jax import lax
from jax.experimental import pallas as pl
from jax.experimental.pallas import tpu as pltpu
from jax.sharding import PartitionSpec as P

MESH = pl.DeviceIdType.MESH
F32 = jnp.float32
BF16 = jnp.bfloat16
NX, NZ = 4, 8
CH = 128


def exact_dot(a, b):
    return jnp.dot(a, b, precision=lax.Precision.HIGHEST, preferred_element_type=F32)


def split(a):
    high = a.astype(BF16)
    return high, (a - high.astype(F32)).astype(BF16)


def split_dot(a, b):
    (ah, al), (bh, bl) = a, b
    one = lambda u, v: jnp.dot(u, v, preferred_element_type=F32)
    return one(ah, bl) + one(al, bh) + one(ah, bh)


def scaled_steps(low, count):
    scales = []
    for _ in range(count):
        scales.append(2.0 / (1.0 + low))
        low = 4.0 * low / (1.0 + low) ** 2
    return scales


class Inverse:
    def __init__(self, a, low, scaled, corrected):
        n = a.shape[0]
        rows = lax.broadcasted_iota(jnp.int32, (n, n), 0)
        cols = lax.broadcasted_iota(jnp.int32, (n, n), 1)
        self.eye = (rows == cols).astype(F32)
        self.unscale = 1.0 / jnp.sqrt(jnp.sum(a * a, axis=(0, 1), keepdims=True))
        self.a = a * self.unscale
        self.scales = scaled_steps(low, scaled)
        self.corrected = corrected
        s = self.scales[0]
        halves = split(self.a)
        self.x = (2.0 * s) * self.eye - (s * s) * self.a
        self.y = (2.0 * s) * self.a - (s * s) * split_dot(halves, halves)

    def run(self, first, last):
        for s in self.scales[first:last]:
            m = split((2.0 * s) * self.eye - (s * s) * self.y)
            self.x, self.y = split_dot(split(self.x), m), split_dot(split(self.y), m)

    def finish(self):
        x = self.x
        for _ in range(self.corrected):
            x = x + split_dot(split(x), split(self.eye - exact_dot(self.a, x)))
        return x * self.unscale


def kernel(
    ridge_conf,
    ridge_hit,
    scores,
    conf_init,
    hit_out,
    conf_out,
    s_buf,
    c_buf,
    z_buf,
    g_acc,
    t_acc,
    g_core,
    g_half,
    g_xy,
    g_z,
    g_full,
    t_core,
    t_xz,
    t_piece,
    t_y,
    t_full,
    known,
    cs, cr, ss, sr, sl, os,
    g1s, g1r, g2s, g2r, g3s, g3r, g4s, g4r,
    h1s, h1r, h2s, h2r, h3s, h3r, h4s, h4r,
):
    own = s_buf.shape[1]
    chunks = own // CH
    hit = lax.axis_index("hit")
    conf = lax.axis_index("conf")
    x = hit // (2 * NZ)
    z = (hit // 2) % NZ
    yh = hit % 2
    yl = conf // 2
    core = conf % 2

    def device(x_, yh_, z_, yl_, core_):
        return ((x_ * NZ + z_) * 2 + yh_, yl_ * 2 + core_)

    y = yh * 2 + yl
    xy = x * 4 + y
    xz = x * NZ + z

    def along_x(r):
        return device((x + r) % NX, yh, z, yl, core)

    def along_y(r):
        p = (y + r) % 4
        return device(x, p // 2, z, p % 2, core)

    def along_z(r):
        return device(x, yh, (z + r) % NZ, yl, core)

    def xy_peer(r, core_):
        p = (xy + r) % 16
        return p, device(p // 4, (p // 2) % 2, z, p % 2, core_)

    def xz_peer(r):
        p = (xz + r) % 32
        return p, device(p // NZ, yh, p % NZ, yl, core)

    group_conf = [conf, yl * 2 + 1 - core, (1 - yl) * 2 + core, (1 - yl) * 2 + 1 - core]
    group = [(hit, c) for c in group_conf]
    beyond = device(x, 1 - yh, z, 1 - yl, core)

    barrier = pltpu.get_barrier_semaphore()
    neighbours = [along_x(1), along_x(3), along_y(1), along_y(3), along_z(1), along_z(NZ - 1)]
    for to in [group[1], group[3]] + neighbours:
        pl.semaphore_signal(barrier, inc=1, device_id=to, device_id_type=MESH)
    pl.semaphore_wait(barrier, 8)

    def tell(k, devices):
        for to in devices:
            pl.semaphore_signal(known.at[k], inc=1, device_id=to, device_id_type=MESH)

    def send(src, dst, send_sem, recv_sem, to):
        return pltpu.make_async_remote_copy(
            src_ref=src, dst_ref=dst, send_sem=send_sem, recv_sem=recv_sem, device_id=to, device_id_type=MESH
        )

    def rows(start, size):
        return pl.ds(pl.multiple_of(start, size), size)

    conf_copies = [send(conf_init, c_buf.at[d], cs.at[d], cr.at[d], to) for d, to in ((1, group[1]), (2, beyond))]
    for copy in conf_copies:
        copy.start()

    def score_copy(d, i):
        return send(
            scores.at[rows(group_conf[d] * own + i * CH, CH)],
            s_buf.at[d, rows(i * CH, CH)],
            ss.at[d, i],
            sr.at[d, i],
            group[d],
        )

    @pl.loop(0, chunks)
    def _(i):
        for d in (2, 3, 1):
            score_copy(d, i).start()

    mine = pltpu.make_async_copy(scores.at[rows(conf * own, own)], s_buf.at[0], sl.at[0])
    mine.start()

    tell(0, neighbours)

    conf_copies[1].wait()
    passed_on = send(c_buf.at[2], c_buf.at[3], cs.at[3], cr.at[3], group[1])
    passed_on.start()
    conf_copies[0].wait()
    c_buf[0] = conf_init[...]
    passed_on.wait()

    def square(m):
        return lax.dot_general(m, m, (((0,), (0,)), ((), ())), preferred_element_type=F32)

    def ridged(gram, ridge):
        n = gram.shape[0]
        r_ = lax.broadcasted_iota(jnp.int32, (n, n), 0)
        c_ = lax.broadcasted_iota(jnp.int32, (n, n), 1)
        return gram + jnp.where(r_ == c_, F32(ridge), F32(0.0))

    gram_conf = (square(c_buf[0]) + square(c_buf[1])) + (square(c_buf[2]) + square(c_buf[3]))
    inverse = Inverse(ridged(gram_conf, ridge_conf), 4.8e-6, 11, 2)
    inverse.run(1, 11)
    g_full[...] = inverse.finish()

    pl.semaphore_wait(known.at[0], 6)
    tell(1, [along_z(2), along_z(NZ - 2)])

    g_acc[...] = jnp.zeros_like(g_acc)
    t_acc[...] = jnp.zeros_like(t_acc)
    mine.wait()

    pl.semaphore_wait(known.at[1], 2)
    tell(2, [along_x(r) for r in (1, 2, 3)])
    pl.semaphore_wait(known.at[2], 3)
    tell(3, [group[1]])
    pl.semaphore_wait(known.at[3], 1)

    def out_copy(i):
        part = rows(i * CH, CH)
        return pltpu.make_async_copy(z_buf.at[part], hit_out.at[part], os.at[i])

    def solve_chunk(i):
        part = rows(i * CH, CH)
        for d in (1, 2, 3):
            score_copy(d, i).wait()
        rhs = jnp.zeros((CH, 256), F32)
        for d in range(4):
            rhs += jnp.dot(s_buf[d, part, :], c_buf[d], preferred_element_type=F32)
        solved = exact_dot(rhs, g_full[...])
        z_buf[part, :] = solved
        out_copy(i).start()
        turned = solved.T.astype(BF16)
        g_acc[...] += jnp.dot(turned, solved.astype(BF16), preferred_element_type=F32)
        return turned

    def add_cross(i, turned):
        part = rows(i * CH, CH)
        for d in range(4):
            t_acc[d % 2, d // 2] += jnp.dot(turned, s_buf[d, part, :], preferred_element_type=F32)

    @pl.loop(0, chunks - 1)
    def _(i):
        add_cross(i, solve_chunk(i))

    turned = solve_chunk(chunks - 1)

    half = rows(core * 128, 128)
    other_half = rows((1 - core) * 128, 128)
    g1 = send(g_acc.at[other_half], g_core, g1s.at[0], g1r.at[0], group[1])
    g1.start()

    add_cross(chunks - 1, turned)
    h1 = send(t_acc.at[1], t_core, h1s.at[0], h1r.at[0], group[1])
    h1.start()

    g1.wait()
    g_half[...] = g_acc[half, :] + g_core[...]

    def g2(r):
        p, to = xy_peer(r, core)
        return send(g_half.at[rows(p * 8, 8)], g_xy.at[r], g2s.at[r], g2r.at[r], to)

    @pl.loop(1, 16)
    def _(r):
        g2(r).start()

    h1.wait()
    t_acc[0] += t_core[...]

    def h2(r):
        p, to = xz_peer(r)
        return send(t_acc.at[0, :, rows(p * 8, 8)], t_xz.at[r], h2s.at[r], h2r.at[r], to)

    @pl.loop(1, 32)
    def _(r):
        h2(r).start()

    g_xy[0] = g_half[rows(xy * 8, 8), :]

    @pl.loop(1, 16)
    def _(r):
        g2(r).wait()

    g_z[z] = jnp.sum(g_xy[...], axis=0)

    def g3(r):
        return send(g_z.at[z], g_z.at[z], g3s.at[r], g3r.at[r], along_z(r))

    @pl.loop(1, NZ)
    def _(r):
        g3(r).start()

    @pl.loop(1, NZ)
    def _(r):
        g3(r).wait()

    kept = rows(core * 128 + xy * 8, 8)
    g_full[kept, :] = jnp.sum(g_z[...], axis=0)

    def g4(r, other):
        to = xy_peer(r, 1 - core if other else core)[1]
        return send(g_full.at[kept], g_full.at[kept], g4s.at[other, r], g4r.at[other, r], to)

    @pl.loop(1, 16)
    def _(r):
        g4(r, 0).start()
        g4(r, 1).start()

    g4(0, 1).start()

    @pl.loop(1, 32)
    def _(r):
        h2(r).wait()

    own_tile = rows(xz * 8, 8)
    t_xz[0] = t_acc[0, :, own_tile, :]
    t_piece[...] = jnp.sum(t_xz[...], axis=0)

    h3 = [
        send(t_piece.at[k], t_y.at[n], h3s.at[n], h3r.at[n], to)
        for n, (k, to) in enumerate([(0, device(x, 1 - yh, z, yl, core)), (1, group[2]), (1, beyond)])
    ]
    for copy in h3:
        copy.start()

    g4(0, 1).wait()

    @pl.loop(1, 16)
    def _(r):
        g4(r, 0).wait()
        g4(r, 1).wait()

    inverse = Inverse(ridged(g_full[...], ridge_hit), 4.9e-7, 12, 2)

    for copy in h3:
        copy.wait()
    t_full[own_tile, :] = (t_piece[0] + t_y[1]) + (t_y[0] + t_y[2])

    def h4(r):
        return send(t_full.at[own_tile], t_full.at[own_tile], h4s.at[r], h4r.at[r], xz_peer(r)[1])

    @pl.loop(1, 32)
    def _(r):
        h4(r).start()

    inverse.run(1, 12)
    solver = inverse.finish()

    @pl.loop(1, 32)
    def _(r):
        h4(r).wait()

    conf_out[...] = split_dot(split(t_full[...].T), split(solver))

    @pl.loop(0, chunks)
    def _(i):
        out_copy(i).wait()


def shards(scores, conf_init):
    hits, confs = scores.shape
    rank = conf_init.shape[1]
    own = hits // 4
    chunks = own // CH
    total_hits = hits * lax.axis_size("hit")
    vmem = pltpu.VMEM
    dma = pltpu.SemaphoreType.DMA

    def body(*refs):
        kernel(0.5, 0.5 * total_hits, *refs)

    return pl.pallas_call(
        body,
        out_shape=(
            jax.ShapeDtypeStruct((own, rank), F32),
            jax.ShapeDtypeStruct((confs, rank), F32),
        ),
        in_specs=[pl.BlockSpec(memory_space=pl.ANY), pl.BlockSpec(memory_space=pltpu.VMEM)],
        out_specs=(pl.BlockSpec(memory_space=pl.ANY), pl.BlockSpec(memory_space=pltpu.VMEM)),
        scratch_shapes=[
            vmem((4, own, confs), BF16),
            vmem((4, confs, rank), BF16),
            vmem((own, rank), F32),
            vmem((rank, rank), F32),
            vmem((2, 2, rank, confs), F32),
            vmem((128, rank), F32),
            vmem((128, rank), F32),
            vmem((16, 8, rank), F32),
            vmem((NZ, 8, rank), F32),
            vmem((rank, rank), F32),
            vmem((2, rank, confs), F32),
            vmem((32, 2, 8, confs), F32),
            vmem((2, 8, confs), F32),
            vmem((3, 8, confs), F32),
            vmem((rank, confs), F32),
            pltpu.SemaphoreType.REGULAR((4,)),
            dma((4,)), dma((4,)), dma((4, chunks)), dma((4, chunks)), dma((1,)), dma((chunks,)),
            dma((1,)), dma((1,)), dma((16,)), dma((16,)), dma((NZ,)), dma((NZ,)), dma((2, 16)), dma((2, 16)),
            dma((1,)), dma((1,)), dma((32,)), dma((32,)), dma((3,)), dma((3,)), dma((32,)), dma((32,)),
        ],
        compiler_params=pltpu.CompilerParams(
            collective_id=0, has_side_effects=True, vmem_limit_bytes=60 * 1024 * 1024
        ),
    )(scores, conf_init)


def solution(mesh):
    return jax.shard_map(
        shards,
        mesh=mesh,
        in_specs=(P("hit", "conf"), P("conf", None)),
        out_specs=(P(("hit", "conf"), None), P("conf", None)),
        check_vma=False,
    )
```

time: 98.4 us -> 86.9 us (0.88)
  Pallas kernels: 92.7 us -> 82.1 us
  local copies, waits for them, and re-layouts: 4.63 us -> 3.4 us
    pallas_call x1, Pallas kernels: 92.7 us -> 82.1 us  [shards(): pl.pallas_call(body, out_shape=(jax.ShapeDtypeStruct((own, rank), F32), j...]
    unnamed x6 -> x4, local copies, waits for them, and re-layouts: 4.63 us -> 3.4 us
where the time goes in v2:
time: 86.9 us; the launch traced here: 86.1 us
  Pallas kernels  82.1 us (94%)
  local copies, waits for them, and re-layouts  3.4 us (4%)
    pallas_call x1, Pallas kernels, shards(): pl.pallas_call(body, out_shape=(jax.ShapeDtypeStruct((own, rank), F32), j...  82.1 us
    unnamed x4, local copies, waits for them, and re-layouts  3.4 us

profile of v2, /device:TPU:6, one launch (start us, length us, event | category | flops | bytes accessed | tf_op | source)
XLA Modules:
  0.0 86.1 jit_solution(4416211641923439877)
XLA Ops:
  0.6 82.1 %shard_map.41 = (f32[1536,256]{1,0:T(8,128)}, f32[256,256]{1,0:T(8,128)}) custom-call(bf16[6144,256]{1,0:T(8,128)(2,1)} %refs_0_.1, bf16[256,256]{1,0:T(8,128)(2,1)} %refs_1_.1), custom_call_target="tpu_custom_call" | custom-call | tf_op jit(solution)/shard_map/pallas_call | solution.py:360
  82.7 0.0 copy-start
  82.7 2.7 %copy.6 = f32[1536,256]{1,0:T(8,128)} copy(f32[1536,256]{1,0:T(8,128)} %get-tuple-element.4) | data formatting | bytes 3145728
  85.4 0.0 copy-done
  85.4 0.7 copy.7
Async XLA Ops:
  82.7 2.7 %copy-start = (f32[256,256]{1,0:T(8,128)S(1)}, f32[256,256]{1,0:T(8,128)}, u32[]{:S(2)}) copy-start(f32[256,256]{1,0:T(8,128)} %get-tuple-element.5) | copy-start | bytes 786436

commit v3 on v2

--- a/solution.py
+++ b/solution.py
@@ -80,14 +80,14 @@
     g_z,
     g_full,
     t_core,
-    t_xz,
-    t_piece,
-    t_y,
+    t_xy,
+    t_part,
+    t_z,
     t_full,
     known,
     cs, cr, ss, sr, sl, os,
-    g1s, g1r, g2s, g2r, g3s, g3r, g4s, g4r,
-    h1s, h1r, h2s, h2r, h3s, h3r, h4s, h4r,
+    g1s, g1r, g2s, g2r, g3s, g3r, g4s, g4r, g5s, g5r,
+    h1s, h1r, h2s, h2r, h3s, h3r, h4s, h4r, h5s, h5r,
 ):
     own = s_buf.shape[1]
     chunks = own // CH
@@ -104,7 +104,6 @@
 
     y = yh * 2 + yl
     xy = x * 4 + y
-    xz = x * NZ + z
 
     def along_x(r):
         return device((x + r) % NX, yh, z, yl, core)
@@ -116,13 +115,9 @@
     def along_z(r):
         return device(x, yh, (z + r) % NZ, yl, core)
 
-    def xy_peer(r, core_):
+    def xy_peer(r):
         p = (xy + r) % 16
-        return p, device(p // 4, (p // 2) % 2, z, p % 2, core_)
-
-    def xz_peer(r):
-        p = (xz + r) % 32
-        return p, device(p // NZ, yh, p % NZ, yl, core)
+        return p, device(p // 4, (p // 2) % 2, z, p % 2, core)
 
     group_conf = [conf, yl * 2 + 1 - core, (1 - yl) * 2 + core, (1 - yl) * 2 + 1 - core]
     group = [(hit, c) for c in group_conf]
@@ -200,8 +195,6 @@
     pl.semaphore_wait(known.at[1], 2)
     tell(2, [along_x(r) for r in (1, 2, 3)])
     pl.semaphore_wait(known.at[2], 3)
-    tell(3, [group[1]])
-    pl.semaphore_wait(known.at[3], 1)
 
     def out_copy(i):
         part = rows(i * CH, CH)
@@ -245,7 +238,7 @@
     g_half[...] = g_acc[half, :] + g_core[...]
 
     def g2(r):
-        p, to = xy_peer(r, core)
+        p, to = xy_peer(r)
         return send(g_half.at[rows(p * 8, 8)], g_xy.at[r], g2s.at[r], g2r.at[r], to)
 
     @pl.loop(1, 16)
@@ -256,10 +249,11 @@
     t_acc[0] += t_core[...]
 
     def h2(r):
-        p, to = xz_peer(r)
-        return send(t_acc.at[0, :, rows(p * 8, 8)], t_xz.at[r], h2s.at[r], h2r.at[r], to)
-
-    @pl.loop(1, 32)
+        p, to = xy_peer(r)
+        block, part = (p + yl) % 2, p // 4 * 2 + p // 2 % 2
+        return send(t_acc.at[0, block, rows(part * 32, 32)], t_xy.at[r], h2s.at[r], h2r.at[r], to)
+
+    @pl.loop(1, 16)
     def _(r):
         h2(r).start()
 
@@ -282,61 +276,89 @@
     def _(r):
         g3(r).wait()
 
-    kept = rows(core * 128 + xy * 8, 8)
-    g_full[kept, :] = jnp.sum(g_z[...], axis=0)
-
-    def g4(r, other):
-        to = xy_peer(r, 1 - core if other else core)[1]
-        return send(g_full.at[kept], g_full.at[kept], g4s.at[other, r], g4r.at[other, r], to)
-
-    @pl.loop(1, 16)
-    def _(r):
-        g4(r, 0).start()
-        g4(r, 1).start()
-
-    g4(0, 1).start()
-
-    @pl.loop(1, 32)
+    def g_rows(p):
+        return rows(core * 128 + p * 8, 8)
+
+    g_full[g_rows(xy), :] = jnp.sum(g_z[...], axis=0)
+
+    def g4(r):
+        return send(g_full.at[g_rows(xy)], g_full.at[g_rows(xy)], g4s.at[r], g4r.at[r], xy_peer(r)[1])
+
+    def g5(r):
+        part = g_rows((xy - r + 16) % 16)
+        return send(g_full.at[part], g_full.at[part], g5s.at[r], g5r.at[r], group[1])
+
+    @pl.loop(1, 16)
+    def _(r):
+        g4(r).start()
+
+    g5(0).start()
+
+    @pl.loop(1, 16)
     def _(r):
         h2(r).wait()
 
-    own_tile = rows(xz * 8, 8)
-    t_xz[0] = t_acc[0, :, own_tile, :]
-    t_piece[...] = jnp.sum(t_xz[...], axis=0)
-
-    h3 = [
-        send(t_piece.at[k], t_y.at[n], h3s.at[n], h3r.at[n], to)
-        for n, (k, to) in enumerate([(0, device(x, 1 - yh, z, yl, core)), (1, group[2]), (1, beyond)])
-    ]
-    for copy in h3:
-        copy.start()
-
-    g4(0, 1).wait()
-
-    @pl.loop(1, 16)
-    def _(r):
-        g4(r, 0).wait()
-        g4(r, 1).wait()
+    part = x * 2 + yh
+    own_rows = rows(part * 32, 32)
+    t_xy[0] = t_acc[0, 0, own_rows, :]
+    t_part[...] = jnp.sum(t_xy[...], axis=0)
+
+    def h3(r):
+        p = (z + r) % NZ
+        tile = t_part.at[rows(p // 2 * 8, 8), rows(p % 2 * 128, 128)]
+        return send(tile, t_z.at[r], h3s.at[r], h3r.at[r], along_z(r))
+
+    @pl.loop(1, NZ)
+    def _(r):
+        h3(r).start()
+
+    @pl.loop(1, 16)
+    def _(r):
+        g4(r).wait()
+        g5(r).start()
+
+    t_z[0] = t_part[rows(z // 2 * 8, 8), rows(z % 2 * 128, 128)]
+
+    @pl.loop(1, NZ)
+    def _(r):
+        h3(r).wait()
+
+    own_tile = (rows(part * 32 + z // 2 * 8, 8), rows(z % 2 * 128, 128))
+    t_full[own_tile] = jnp.sum(t_z[...], axis=0)
+
+    def h4(r):
+        return send(t_full.at[own_tile], t_full.at[own_tile], h4s.at[r], h4r.at[r], along_z(r))
+
+    @pl.loop(1, NZ)
+    def _(r):
+        h4(r).start()
+
+    @pl.loop(0, 16)
+    def _(r):
+        g5(r).wait()
 
     inverse = Inverse(ridged(g_full[...], ridge_hit), 4.9e-7, 12, 2)
-
-    for copy in h3:
-        copy.wait()
-    t_full[own_tile, :] = (t_piece[0] + t_y[1]) + (t_y[0] + t_y[2])
-
-    def h4(r):
-        return send(t_full.at[own_tile], t_full.at[own_tile], h4s.at[r], h4r.at[r], xz_peer(r)[1])
-
-    @pl.loop(1, 32)
-    def _(r):
-        h4(r).start()
-
-    inverse.run(1, 12)
+    inverse.run(1, 6)
+
+    @pl.loop(1, NZ)
+    def _(r):
+        h4(r).wait()
+
+    def h5(r):
+        p = (part + r) % 8
+        to = device(p // 2, p % 2, z, yl, core)
+        return send(t_full.at[own_rows], t_full.at[own_rows], h5s.at[r], h5r.at[r], to)
+
+    @pl.loop(1, 8)
+    def _(r):
+        h5(r).start()
+
+    inverse.run(6, 12)
     solver = inverse.finish()
 
-    @pl.loop(1, 32)
-    def _(r):
-        h4(r).wait()
+    @pl.loop(1, 8)
+    def _(r):
+        h5(r).wait()
 
     conf_out[...] = split_dot(split(t_full[...].T), split(solver))
 
@@ -377,14 +399,14 @@
             vmem((NZ, 8, rank), F32),
             vmem((rank, rank), F32),
             vmem((2, rank, confs), F32),
-            vmem((32, 2, 8, confs), F32),
-            vmem((2, 8, confs), F32),
-            vmem((3, 8, confs), F32),
+            vmem((16, 32, confs), F32),
+            vmem((32, confs), F32),
+            vmem((NZ, 8, 128), F32),
             vmem((rank, confs), F32),
-            pltpu.SemaphoreType.REGULAR((4,)),
+            pltpu.SemaphoreType.REGULAR((3,)),
             dma((4,)), dma((4,)), dma((4, chunks)), dma((4, chunks)), dma((1,)), dma((chunks,)),
-            dma((1,)), dma((1,)), dma((16,)), dma((16,)), dma((NZ,)), dma((NZ,)), dma((2, 16)), dma((2, 16)),
-            dma((1,)), dma((1,)), dma((32,)), dma((32,)), dma((3,)), dma((3,)), dma((32,)), dma((32,)),
+            dma((1,)), dma((1,)), dma((16,)), dma((16,)), dma((NZ,)), dma((NZ,)), dma((16,)), dma((16,)), dma((16,)), dma((16,)),
+            dma((1,)), dma((1,)), dma((16,)), dma((16,)), dma((NZ,)), dma((NZ,)), dma((NZ,)), dma((NZ,)), dma((8,)), dma((8,)),
         ],
         compiler_params=pltpu.CompilerParams(
             collective_id=0, has_side_effects=True, vmem_limit_bytes=60 * 1024 * 1024

time: 86.9 us -> 83.1 us (0.956)
  Pallas kernels: 82.1 us -> 78.3 us
    pallas_call x1, Pallas kernels: 82.1 us -> 78.3 us  [shards(): pl.pallas_call(body, out_shape=(jax.ShapeDtypeStruct((own, rank), F32), j...]
where the time goes in v3:
time: 83.1 us; the launch traced here: 82.3 us
  Pallas kernels  78.3 us (94%)
  local copies, waits for them, and re-layouts  3.4 us (4%)
    pallas_call x1, Pallas kernels, shards(): pl.pallas_call(body, out_shape=(jax.ShapeDtypeStruct((own, rank), F32), j...  78.3 us
    unnamed x4, local copies, waits for them, and re-layouts  3.4 us

profile of v3, /device:TPU:6, one launch (start us, length us, event | category | flops | bytes accessed | tf_op | source)
XLA Modules:
  0.0 82.3 jit_solution(10619374487064093085)
XLA Ops:
  0.6 78.3 %shard_map.41 = (f32[1536,256]{1,0:T(8,128)}, f32[256,256]{1,0:T(8,128)}) custom-call(bf16[6144,256]{1,0:T(8,128)(2,1)} %refs_0_.1, bf16[256,256]{1,0:T(8,128)(2,1)} %refs_1_.1), custom_call_target="tpu_custom_call" | custom-call | tf_op jit(solution)/shard_map/pallas_call | solution.py:382
  78.9 0.0 copy-start
  78.9 2.7 %copy.6 = f32[1536,256]{1,0:T(8,128)} copy(f32[1536,256]{1,0:T(8,128)} %get-tuple-element.4) | data formatting | bytes 3145728
  81.6 0.0 copy-done
  81.6 0.7 copy.7
Async XLA Ops:
  78.9 2.7 %copy-start = (f32[256,256]{1,0:T(8,128)S(1)}, f32[256,256]{1,0:T(8,128)}, u32[]{:S(2)}) copy-start(f32[256,256]{1,0:T(8,128)} %get-tuple-element.5) | copy-start | bytes 786436

commit v4 on v3

--- a/solution.py
+++ b/solution.py
@@ -10,6 +10,7 @@
 BF16 = jnp.bfloat16
 NX, NZ = 4, 8
 CH = 128
+PARTS = 4
 
 
 def exact_dot(a, b):
@@ -68,7 +69,8 @@
     scores,
     conf_init,
     hit_out,
-    conf_out,
+    t_full,
+    solver_out,
     s_buf,
     c_buf,
     z_buf,
@@ -83,7 +85,6 @@
     t_xy,
     t_part,
     t_z,
-    t_full,
     known,
     cs, cr, ss, sr, sl, os,
     g1s, g1r, g2s, g2r, g3s, g3r, g4s, g4r, g5s, g5r,
@@ -312,33 +313,32 @@
     def _(r):
         h3(r).start()
 
+    t_z[0] = t_part[rows(z // 2 * 8, 8), rows(z % 2 * 128, 128)]
+
+    @pl.loop(1, NZ)
+    def _(r):
+        h3(r).wait()
+
+    own_tile = (rows(part * 32 + z // 2 * 8, 8), rows(z % 2 * 128, 128))
+    t_full[own_tile] = jnp.sum(t_z[...], axis=0)
+
+    def h4(r):
+        return send(t_full.at[own_tile], t_full.at[own_tile], h4s.at[r], h4r.at[r], along_z(r))
+
+    @pl.loop(1, NZ)
+    def _(r):
+        h4(r).start()
+
     @pl.loop(1, 16)
     def _(r):
         g4(r).wait()
         g5(r).start()
 
-    t_z[0] = t_part[rows(z // 2 * 8, 8), rows(z % 2 * 128, 128)]
-
-    @pl.loop(1, NZ)
-    def _(r):
-        h3(r).wait()
-
-    own_tile = (rows(part * 32 + z // 2 * 8, 8), rows(z % 2 * 128, 128))
-    t_full[own_tile] = jnp.sum(t_z[...], axis=0)
-
-    def h4(r):
-        return send(t_full.at[own_tile], t_full.at[own_tile], h4s.at[r], h4r.at[r], along_z(r))
-
-    @pl.loop(1, NZ)
-    def _(r):
-        h4(r).start()
-
     @pl.loop(0, 16)
     def _(r):
         g5(r).wait()
 
     inverse = Inverse(ridged(g_full[...], ridge_hit), 4.9e-7, 12, 2)
-    inverse.run(1, 6)
 
     @pl.loop(1, NZ)
     def _(r):
@@ -353,18 +353,29 @@
     def _(r):
         h5(r).start()
 
-    inverse.run(6, 12)
-    solver = inverse.finish()
+    inverse.run(1, 12)
+    solver_out[...] = inverse.finish()
 
     @pl.loop(1, 8)
     def _(r):
         h5(r).wait()
-
-    conf_out[...] = split_dot(split(t_full[...].T), split(solver))
 
     @pl.loop(0, chunks)
     def _(i):
         out_copy(i).wait()
+
+
+def results(hit_in, rhs_conf, solver, hit_out, conf_out, sems):
+    size = hit_in.shape[0] // PARTS
+    copies = [
+        pltpu.make_async_copy(hit_in.at[pl.ds(i * size, size)], hit_out.at[pl.ds(i * size, size)], sems.at[i])
+        for i in range(PARTS)
+    ]
+    for copy in copies:
+        copy.start()
+    conf_out[...] = split_dot(split(rhs_conf[...].T), split(solver[...]))
+    for copy in copies:
+        copy.wait()
 
 
 def shards(scores, conf_init):
@@ -379,14 +390,16 @@
     def body(*refs):
         kernel(0.5, 0.5 * total_hits, *refs)
 
-    return pl.pallas_call(
+    in_hbm, in_vmem = pl.BlockSpec(memory_space=pl.ANY), pl.BlockSpec(memory_space=pltpu.VMEM)
+    hit_factors, rhs_conf, solver = pl.pallas_call(
         body,
         out_shape=(
             jax.ShapeDtypeStruct((own, rank), F32),
-            jax.ShapeDtypeStruct((confs, rank), F32),
+            jax.ShapeDtypeStruct((rank, confs), F32),
+            jax.ShapeDtypeStruct((rank, rank), F32),
         ),
-        in_specs=[pl.BlockSpec(memory_space=pl.ANY), pl.BlockSpec(memory_space=pltpu.VMEM)],
-        out_specs=(pl.BlockSpec(memory_space=pl.ANY), pl.BlockSpec(memory_space=pltpu.VMEM)),
+        in_specs=[in_hbm, in_vmem],
+        out_specs=(in_hbm, in_vmem, in_vmem),
         scratch_shapes=[
             vmem((4, own, confs), BF16),
             vmem((4, confs, rank), BF16),
@@ -402,7 +415,6 @@
             vmem((16, 32, confs), F32),
             vmem((32, confs), F32),
             vmem((NZ, 8, 128), F32),
-            vmem((rank, confs), F32),
             pltpu.SemaphoreType.REGULAR((3,)),
             dma((4,)), dma((4,)), dma((4, chunks)), dma((4, chunks)), dma((1,)), dma((chunks,)),
             dma((1,)), dma((1,)), dma((16,)), dma((16,)), dma((NZ,)), dma((NZ,)), dma((16,)), dma((16,)), dma((16,)), dma((16,)),
@@ -412,6 +424,17 @@
             collective_id=0, has_side_effects=True, vmem_limit_bytes=60 * 1024 * 1024
         ),
     )(scores, conf_init)
+    return pl.pallas_call(
+        results,
+        out_shape=(
+            jax.ShapeDtypeStruct((own, rank), F32),
+            jax.ShapeDtypeStruct((confs, rank), F32),
+        ),
+        in_specs=[in_hbm, in_vmem, in_vmem],
+        out_specs=(in_hbm, in_vmem),
+        scratch_shapes=[dma((PARTS,))],
+        compiler_params=pltpu.CompilerParams(vmem_limit_bytes=60 * 1024 * 1024),
+    )(hit_factors, rhs_conf, solver)
 
 
 def solution(mesh):

time: 83.1 us -> 129 us (1.55)
  Pallas kernels: 78.3 us -> 128 us
  local copies, waits for them, and re-layouts: 3.4 us -> 0 us
    pallas_call x0 -> x1, Pallas kernels: none -> 50.5 us  [shards(): pl.pallas_call(results, out_shape=(jax.ShapeDtypeStruct((own, rank), F32)...]
    unnamed x4 -> x0, local copies, waits for them, and re-layouts: 3.4 us -> none
where the time goes in v4:
time: 129 us
  Pallas kernels  128 us (99%)
    pallas_call x1, Pallas kernels, shards(): pl.pallas_call(body, out_shape=(jax.ShapeDtypeStruct((own, rank), F32), j...  77.6 us
    pallas_call x1, Pallas kernels, shards(): pl.pallas_call(results, out_shape=(jax.ShapeDtypeStruct((own, rank), F32)...  50.5 us

profile of v4, /device:TPU:6, one launch (start us, length us, event | category | flops | bytes accessed | tf_op | source)
XLA Modules:
  0.0 128.8 jit_solution(12945364554661362927)
XLA Ops:
  0.6 77.6 %shard_map.41 = (f32[1536,256]{1,0:T(8,128)}, f32[256,256]{1,0:T(8,128)}, f32[256,256]{1,0:T(8,128)}) custom-call(bf16[6144,256]{1,0:T(8,128)(2,1)} %refs_0_.1, bf16[256,256]{1,0:T(8,128)(2,1)} %refs_1_.1), custom_call_target="tpu_custom_call" | custom-call | tf_op jit(solution)/shard_map/pallas_call | solution.py:394
  78.3 50.5 %shard_map.42 = (f32[1536,256]{1,0:T(8,128)}, f32[256,256]{1,0:T(8,128)}) custom-call(f32[1536,256]{1,0:T(8,128)} %get-tuple-element.5.hit_in, f32[256,256]{1,0:T(8,128)} %get-tuple-element.6.rhs_conf, f32[256,256]{1,0:T(8,128)} %get-tuple-element.7.solver), custom_call_target="tpu_custom_call" | custom-call | tf_op jit(solution)/shard_map/pallas_call | solution.py:427

commit v5 on v3

--- a/solution.py
+++ b/solution.py
@@ -312,33 +312,32 @@
     def _(r):
         h3(r).start()
 
+    t_z[0] = t_part[rows(z // 2 * 8, 8), rows(z % 2 * 128, 128)]
+
+    @pl.loop(1, NZ)
+    def _(r):
+        h3(r).wait()
+
+    own_tile = (rows(part * 32 + z // 2 * 8, 8), rows(z % 2 * 128, 128))
+    t_full[own_tile] = jnp.sum(t_z[...], axis=0)
+
+    def h4(r):
+        return send(t_full.at[own_tile], t_full.at[own_tile], h4s.at[r], h4r.at[r], along_z(r))
+
+    @pl.loop(1, NZ)
+    def _(r):
+        h4(r).start()
+
     @pl.loop(1, 16)
     def _(r):
         g4(r).wait()
         g5(r).start()
 
-    t_z[0] = t_part[rows(z // 2 * 8, 8), rows(z % 2 * 128, 128)]
-
-    @pl.loop(1, NZ)
-    def _(r):
-        h3(r).wait()
-
-    own_tile = (rows(part * 32 + z // 2 * 8, 8), rows(z % 2 * 128, 128))
-    t_full[own_tile] = jnp.sum(t_z[...], axis=0)
-
-    def h4(r):
-        return send(t_full.at[own_tile], t_full.at[own_tile], h4s.at[r], h4r.at[r], along_z(r))
-
-    @pl.loop(1, NZ)
-    def _(r):
-        h4(r).start()
-
     @pl.loop(0, 16)
     def _(r):
         g5(r).wait()
 
     inverse = Inverse(ridged(g_full[...], ridge_hit), 4.9e-7, 12, 2)
-    inverse.run(1, 6)
 
     @pl.loop(1, NZ)
     def _(r):
@@ -353,7 +352,7 @@
     def _(r):
         h5(r).start()
 
-    inverse.run(6, 12)
+    inverse.run(1, 12)
     solver = inverse.finish()
 
     @pl.loop(1, 8)
@@ -379,14 +378,15 @@
     def body(*refs):
         kernel(0.5, 0.5 * total_hits, *refs)
 
+    in_hbm, in_vmem = pl.BlockSpec(memory_space=pl.ANY), pl.BlockSpec(memory_space=pltpu.VMEM)
     return pl.pallas_call(
         body,
         out_shape=(
             jax.ShapeDtypeStruct((own, rank), F32),
             jax.ShapeDtypeStruct((confs, rank), F32),
         ),
-        in_specs=[pl.BlockSpec(memory_space=pl.ANY), pl.BlockSpec(memory_space=pltpu.VMEM)],
-        out_specs=(pl.BlockSpec(memory_space=pl.ANY), pl.BlockSpec(memory_space=pltpu.VMEM)),
+        in_specs=[in_hbm, in_vmem],
+        out_specs=(in_hbm, in_vmem),
         scratch_shapes=[
             vmem((4, own, confs), BF16),
             vmem((4, confs, rank), BF16),
@@ -409,10 +409,9 @@
             dma((1,)), dma((1,)), dma((16,)), dma((16,)), dma((NZ,)), dma((NZ,)), dma((NZ,)), dma((NZ,)), dma((8,)), dma((8,)),
         ],
         compiler_params=pltpu.CompilerParams(
-            collective_id=0, has_side_effects=True, vmem_limit_bytes=60 * 1024 * 1024
+            collective_id=0, has_side_effects=True, vmem_limit_bytes=51 * 1024 * 1024
         ),
     )(scores, conf_init)
-
 
 def solution(mesh):
     return jax.shard_map(

time: 83.1 us -> 79.9 us (0.961)
  Pallas kernels: 78.3 us -> 76.4 us
    pallas_call x1, Pallas kernels: 78.3 us -> 76.4 us  [shards(): pl.pallas_call(body, out_shape=(jax.ShapeDtypeStruct((own, rank), F32), j...]
where the time goes in v5:
time: 79.9 us; the launch traced here: 79.8 us
  Pallas kernels  76.4 us (96%)
  local copies, waits for them, and re-layouts  2.74 us (3%)
    pallas_call x1, Pallas kernels, shards(): pl.pallas_call(body, out_shape=(jax.ShapeDtypeStruct((own, rank), F32), j...  76.4 us
    unnamed x4, local copies, waits for them, and re-layouts  2.74 us

profile of v5, /device:TPU:6, one launch (start us, length us, event | category | flops | bytes accessed | tf_op | source)
XLA Modules:
  0.0 79.8 jit_solution(12321537218710880722)
XLA Ops:
  0.6 0.0 copy-start
  0.6 0.9 %copy-done = bf16[256,256]{1,0:T(8,128)(2,1)S(1)} copy-done((bf16[256,256]{1,0:T(8,128)(2,1)S(1)}, bf16[256,256]{1,0:T(8,128)(2,1)}, u32[]{:S(2)}) %copy-start) | copy-done | bytes 131096
  1.5 76.4 %shard_map.41 = (f32[1536,256]{1,0:T(8,128)S(1)}, f32[256,256]{1,0:T(8,128)S(1)}) custom-call(bf16[6144,256]{1,0:T(8,128)(2,1)} %refs_0_.1, bf16[256,256]{1,0:T(8,128)(2,1)S(1)} %copy-done), custom_call_target="tpu_custom_call" | custom-call | tf_op jit(solution)/shard_map/pallas_call | solution.py:382
  77.9 1.1 %copy.6 = f32[1536,256]{1,0:T(8,128)} copy(f32[1536,256]{1,0:T(8,128)S(1)} %get-tuple-element.4) | data formatting | bytes 3145728
  79.1 0.7 copy.7
Async XLA Ops:
  0.6 0.9 %copy-start = (bf16[256,256]{1,0:T(8,128)(2,1)S(1)}, bf16[256,256]{1,0:T(8,128)(2,1)}, u32[]{:S(2)}) copy-start(bf16[256,256]{1,0:T(8,128)(2,1)} %refs_1_.1) | copy-start | bytes 393220

commit v6 on v5

--- a/solution.py
+++ b/solution.py
@@ -81,13 +81,12 @@
     g_full,
     t_core,
     t_xy,
-    t_part,
     t_z,
     t_full,
     known,
     cs, cr, ss, sr, sl, os,
     g1s, g1r, g2s, g2r, g3s, g3r, g4s, g4r, g5s, g5r,
-    h1s, h1r, h2s, h2r, h3s, h3r, h4s, h4r, h5s, h5r,
+    h1s, h1r, h2s, h2r, h3s, h3r, h4s, h4r,
 ):
     own = s_buf.shape[1]
     chunks = own // CH
@@ -301,32 +300,14 @@
     part = x * 2 + yh
     own_rows = rows(part * 32, 32)
     t_xy[0] = t_acc[0, 0, own_rows, :]
-    t_part[...] = jnp.sum(t_xy[...], axis=0)
+    t_z[z] = jnp.sum(t_xy[...], axis=0)
 
     def h3(r):
-        p = (z + r) % NZ
-        tile = t_part.at[rows(p // 2 * 8, 8), rows(p % 2 * 128, 128)]
-        return send(tile, t_z.at[r], h3s.at[r], h3r.at[r], along_z(r))
+        return send(t_z.at[z], t_z.at[z], h3s.at[r], h3r.at[r], along_z(r))
 
     @pl.loop(1, NZ)
     def _(r):
         h3(r).start()
-
-    t_z[0] = t_part[rows(z // 2 * 8, 8), rows(z % 2 * 128, 128)]
-
-    @pl.loop(1, NZ)
-    def _(r):
-        h3(r).wait()
-
-    own_tile = (rows(part * 32 + z // 2 * 8, 8), rows(z % 2 * 128, 128))
-    t_full[own_tile] = jnp.sum(t_z[...], axis=0)
-
-    def h4(r):
-        return send(t_full.at[own_tile], t_full.at[own_tile], h4s.at[r], h4r.at[r], along_z(r))
-
-    @pl.loop(1, NZ)
-    def _(r):
-        h4(r).start()
 
     @pl.loop(1, 16)
     def _(r):
@@ -337,27 +318,29 @@
     def _(r):
         g5(r).wait()
 
-    inverse = Inverse(ridged(g_full[...], ridge_hit), 4.9e-7, 12, 2)
+    inverse = Inverse(ridged(g_full[...], ridge_hit), 4.9e-7, 11, 2)
 
     @pl.loop(1, NZ)
     def _(r):
-        h4(r).wait()
-
-    def h5(r):
+        h3(r).wait()
+
+    t_full[own_rows, :] = jnp.sum(t_z[...], axis=0)
+
+    def h4(r):
         p = (part + r) % 8
         to = device(p // 2, p % 2, z, yl, core)
-        return send(t_full.at[own_rows], t_full.at[own_rows], h5s.at[r], h5r.at[r], to)
+        return send(t_full.at[own_rows], t_full.at[own_rows], h4s.at[r], h4r.at[r], to)
 
     @pl.loop(1, 8)
     def _(r):
-        h5(r).start()
-
-    inverse.run(1, 12)
+        h4(r).start()
+
+    inverse.run(1, 11)
     solver = inverse.finish()
 
     @pl.loop(1, 8)
     def _(r):
-        h5(r).wait()
+        h4(r).wait()
 
     conf_out[...] = split_dot(split(t_full[...].T), split(solver))
 
@@ -400,13 +383,12 @@
             vmem((rank, rank), F32),
             vmem((2, rank, confs), F32),
             vmem((16, 32, confs), F32),
-            vmem((32, confs), F32),
-            vmem((NZ, 8, 128), F32),
+            vmem((NZ, 32, confs), F32),
             vmem((rank, confs), F32),
             pltpu.SemaphoreType.REGULAR((3,)),
             dma((4,)), dma((4,)), dma((4, chunks)), dma((4, chunks)), dma((1,)), dma((chunks,)),
             dma((1,)), dma((1,)), dma((16,)), dma((16,)), dma((NZ,)), dma((NZ,)), dma((16,)), dma((16,)), dma((16,)), dma((16,)),
-            dma((1,)), dma((1,)), dma((16,)), dma((16,)), dma((NZ,)), dma((NZ,)), dma((NZ,)), dma((NZ,)), dma((8,)), dma((8,)),
+            dma((1,)), dma((1,)), dma((16,)), dma((16,)), dma((NZ,)), dma((NZ,)), dma((8,)), dma((8,)),
         ],
         compiler_params=pltpu.CompilerParams(
             collective_id=0, has_side_effects=True, vmem_limit_bytes=51 * 1024 * 1024

time: 79.9 us -> 78.7 us (0.985)
  Pallas kernels: 76.4 us -> 75.1 us
    pallas_call x1, Pallas kernels: 76.4 us -> 75.1 us  [shards(): pl.pallas_call(body, out_shape=(jax.ShapeDtypeStruct((own, rank), F32), j...]
where the time goes in v6:
time: 78.7 us; the launch traced here: 78.5 us
  Pallas kernels  75.1 us (95%)
  local copies, waits for them, and re-layouts  2.74 us (3%)
    pallas_call x1, Pallas kernels, shards(): pl.pallas_call(body, out_shape=(jax.ShapeDtypeStruct((own, rank), F32), j...  75.1 us
    unnamed x4, local copies, waits for them, and re-layouts  2.74 us

profile of v6, /device:TPU:6, one launch (start us, length us, event | category | flops | bytes accessed | tf_op | source)
XLA Modules:
  0.0 78.5 jit_solution(11194956486714777948)
XLA Ops:
  0.6 0.0 copy-start
  0.6 0.9 %copy-done = bf16[256,256]{1,0:T(8,128)(2,1)S(1)} copy-done((bf16[256,256]{1,0:T(8,128)(2,1)S(1)}, bf16[256,256]{1,0:T(8,128)(2,1)}, u32[]{:S(2)}) %copy-start) | copy-done | bytes 131096
  1.5 75.1 %shard_map.41 = (f32[1536,256]{1,0:T(8,128)S(1)}, f32[256,256]{1,0:T(8,128)S(1)}) custom-call(bf16[6144,256]{1,0:T(8,128)(2,1)} %refs_0_.1, bf16[256,256]{1,0:T(8,128)(2,1)S(1)} %copy-done), custom_call_target="tpu_custom_call" | custom-call | tf_op jit(solution)/shard_map/pallas_call | solution.py:365
  76.7 1.1 %copy.6 = f32[1536,256]{1,0:T(8,128)} copy(f32[1536,256]{1,0:T(8,128)S(1)} %get-tuple-element.4) | data formatting | bytes 3145728
  77.8 0.7 copy.7
Async XLA Ops:
  0.6 0.9 %copy-start = (bf16[256,256]{1,0:T(8,128)(2,1)S(1)}, bf16[256,256]{1,0:T(8,128)(2,1)}, u32[]{:S(2)}) copy-start(bf16[256,256]{1,0:T(8,128)(2,1)} %refs_1_.1) | copy-start | bytes 393220

commit v7 on v6

--- a/solution.py
+++ b/solution.py
@@ -318,7 +318,7 @@
     def _(r):
         g5(r).wait()
 
-    inverse = Inverse(ridged(g_full[...], ridge_hit), 4.9e-7, 11, 2)
+    inverse = Inverse(ridged(g_full[...], ridge_hit), 4.9e-7, 12, 2)
 
     @pl.loop(1, NZ)
     def _(r):
@@ -335,7 +335,7 @@
     def _(r):
         h4(r).start()
 
-    inverse.run(1, 11)
+    inverse.run(1, 12)
     solver = inverse.finish()
 
     @pl.loop(1, 8)

time: 78.7 us -> 79 us (level)
  no operation moved by 1% of the time
where the time goes in v7:
time: 79 us; the launch traced here: 78.9 us
  Pallas kernels  75.5 us (96%)
  local copies, waits for them, and re-layouts  2.74 us (3%)
    pallas_call x1, Pallas kernels, shards(): pl.pallas_call(body, out_shape=(jax.ShapeDtypeStruct((own, rank), F32), j...  75.5 us
    unnamed x4, local copies, waits for them, and re-layouts  2.74 us

profile of v7, /device:TPU:6, one launch (start us, length us, event | category | flops | bytes accessed | tf_op | source)
XLA Modules:
  0.0 78.9 jit_solution(16554691054091967902)
XLA Ops:
  0.6 0.0 copy-start
  0.6 0.9 %copy-done = bf16[256,256]{1,0:T(8,128)(2,1)S(1)} copy-done((bf16[256,256]{1,0:T(8,128)(2,1)S(1)}, bf16[256,256]{1,0:T(8,128)(2,1)}, u32[]{:S(2)}) %copy-start) | copy-done | bytes 131096
  1.5 75.5 %shard_map.41 = (f32[1536,256]{1,0:T(8,128)S(1)}, f32[256,256]{1,0:T(8,128)S(1)}) custom-call(bf16[6144,256]{1,0:T(8,128)(2,1)} %refs_0_.1, bf16[256,256]{1,0:T(8,128)(2,1)S(1)} %copy-done), custom_call_target="tpu_custom_call" | custom-call | tf_op jit(solution)/shard_map/pallas_call | solution.py:365
  77.0 1.1 %copy.6 = f32[1536,256]{1,0:T(8,128)} copy(f32[1536,256]{1,0:T(8,128)S(1)} %get-tuple-element.4) | data formatting | bytes 3145728
  78.2 0.7 copy.7
Async XLA Ops:
  0.6 0.9 %copy-start = (bf16[256,256]{1,0:T(8,128)(2,1)S(1)}, bf16[256,256]{1,0:T(8,128)(2,1)}, u32[]{:S(2)}) copy-start(bf16[256,256]{1,0:T(8,128)(2,1)} %refs_1_.1) | copy-start | bytes 393220

commit v8 on v7

--- a/solution.py
+++ b/solution.py
@@ -83,6 +83,7 @@
     t_xy,
     t_z,
     t_full,
+    g_inv,
     known,
     cs, cr, ss, sr, sl, os,
     g1s, g1r, g2s, g2r, g3s, g3r, g4s, g4r, g5s, g5r,
@@ -182,7 +183,7 @@
     gram_conf = (square(c_buf[0]) + square(c_buf[1])) + (square(c_buf[2]) + square(c_buf[3]))
     inverse = Inverse(ridged(gram_conf, ridge_conf), 4.8e-6, 11, 2)
     inverse.run(1, 11)
-    g_full[...] = inverse.finish()
+    g_inv[0], g_inv[1] = split(inverse.finish())
 
     pl.semaphore_wait(known.at[0], 6)
     tell(1, [along_z(2), along_z(NZ - 2)])
@@ -206,7 +207,7 @@
         rhs = jnp.zeros((CH, 256), F32)
         for d in range(4):
             rhs += jnp.dot(s_buf[d, part, :], c_buf[d], preferred_element_type=F32)
-        solved = exact_dot(rhs, g_full[...])
+        solved = split_dot(split(rhs), (g_inv[0], g_inv[1]))
         z_buf[part, :] = solved
         out_copy(i).start()
         turned = solved.T.astype(BF16)
@@ -385,6 +386,7 @@
             vmem((16, 32, confs), F32),
             vmem((NZ, 32, confs), F32),
             vmem((rank, confs), F32),
+            vmem((2, rank, rank), BF16),
             pltpu.SemaphoreType.REGULAR((3,)),
             dma((4,)), dma((4,)), dma((4, chunks)), dma((4, chunks)), dma((1,)), dma((chunks,)),
             dma((1,)), dma((1,)), dma((16,)), dma((16,)), dma((NZ,)), dma((NZ,)), dma((16,)), dma((16,)), dma((16,)), dma((16,)),

time: 79 us -> 78.9 us (level)
  no operation moved by 1% of the time
where the time goes in v8:
time: 78.9 us; the launch traced here: 78.8 us
  Pallas kernels  75.4 us (96%)
  local copies, waits for them, and re-layouts  2.74 us (3%)
    pallas_call x1, Pallas kernels, shards(): pl.pallas_call(body, out_shape=(jax.ShapeDtypeStruct((own, rank), F32), j...  75.4 us
    unnamed x4, local copies, waits for them, and re-layouts  2.74 us

profile of v8, /device:TPU:6, one launch (start us, length us, event | category | flops | bytes accessed | tf_op | source)
XLA Modules:
  0.0 78.8 jit_solution(2862429377487481768)
XLA Ops:
  0.6 0.0 copy-start
  0.6 0.9 %copy-done = bf16[256,256]{1,0:T(8,128)(2,1)S(1)} copy-done((bf16[256,256]{1,0:T(8,128)(2,1)S(1)}, bf16[256,256]{1,0:T(8,128)(2,1)}, u32[]{:S(2)}) %copy-start) | copy-done | bytes 131096
  1.5 75.4 %shard_map.41 = (f32[1536,256]{1,0:T(8,128)S(1)}, f32[256,256]{1,0:T(8,128)S(1)}) custom-call(bf16[6144,256]{1,0:T(8,128)(2,1)} %refs_0_.1, bf16[256,256]{1,0:T(8,128)(2,1)S(1)} %copy-done), custom_call_target="tpu_custom_call" | custom-call | tf_op jit(solution)/shard_map/pallas_call | solution.py:366
  76.9 1.1 %copy.6 = f32[1536,256]{1,0:T(8,128)} copy(f32[1536,256]{1,0:T(8,128)S(1)} %get-tuple-element.4) | data formatting | bytes 3145728
  78.1 0.7 copy.7
Async XLA Ops:
  0.6 0.9 %copy-start = (bf16[256,256]{1,0:T(8,128)(2,1)S(1)}, bf16[256,256]{1,0:T(8,128)(2,1)}, u32[]{:S(2)}) copy-start(bf16[256,256]{1,0:T(8,128)(2,1)} %refs_1_.1) | copy-start | bytes 393220
